TPU v7x, 32 devices: a whole 2x2x4 slice. The times are simulated.
32 devices in a mesh: dom: 2 (over y), grp: 16 (over z, x, core).
Axes of the slice: x: 2, y: 2, z: 4, core: 2. Of those that a mesh axis runs over, the one named last changes fastest.
Arguments:
- routes: int32 [2048, 8], P(('dom', 'grp')), parts along dimension 0, may hold values from 0 to 15, as said below
- gates: float32 [2048, 8], P(('dom', 'grp')), parts along dimension 0, may hold values from 0.05 to 0.6
- hidden: bfloat16 [2048, 8, 1024], P(('dom', 'grp')), parts along dimension 0, may hold values from -6 to 6
- expert_weight: bfloat16 [16, 1024, 3584], P('grp'), may hold values from -0.1875 to 0.1875
- shared_out: bfloat16 [2048, 3584], P(('dom', 'grp')), parts along dimension 0, may hold values from -6 to 6
Outputs:
- combined: bfloat16 [2048, 3584], P(('dom', 'grp')), parts along dimension 0
There are 2 independent parts, one for each index of `dom`. A program takes and returns all parts, laid end to end along the dimension named above; an argument that names none is the same for every part. Nothing has to cross between parts.
Inputs may be any that keep to these rules, and one draw needn't show every extreme that they name: `routes`: each token names 8 different experts, 4 in each of 2 different groups (2 is the smaller of 4 and 2; the group of expert e is e // 8). Among the 64 tokens of one device every group is named by exactly 64 tokens, no expert is named by more than 64 tokens, and one expert exactly 64 times.
All inputs are finite; a program needn't handle non-finite values.
Results may differ from a plain program's by a relative error of at most 0.0065.
Values may be sent and summed in bfloat16 or wider, within the bound.
A program may use at most 64 MiB of HBM per device.

v0:
```python
import jax
import jax.numpy as jnp
from jax import lax
from jax.sharding import PartitionSpec as P

TOPG = 4
GROUP_DEV = 8


def per_device(routes, gates, hidden, expert_weight, shared_out):
    tokens_here = routes.shape[0]
    top_slots = routes.shape[1]
    hidden_width = hidden.shape[2]
    out_width = expert_weight.shape[2]
    experts = lax.axis_size("grp") * expert_weight.shape[0]
    groups = lax.axis_size("grp") // GROUP_DEV
    group_share = tokens_here * min(TOPG, groups) // groups
    capacity = min(group_share, max(2, 2 * tokens_here * top_slots // experts))
    expert_ids = routes.reshape(-1)
    onehot = (expert_ids[:, None] == jnp.arange(experts, dtype=jnp.int32)[None, :]).astype(
        jnp.int32
    )
    slot_index = jnp.sum((jnp.cumsum(onehot, axis=0) - onehot) * onehot, axis=1)
    flat_rows = hidden.reshape(-1, hidden_width)
    outgoing = (
        jnp.zeros((experts, capacity, hidden_width), jnp.bfloat16)
        .at[expert_ids, slot_index]
        .set(flat_rows)
    )
    weight = expert_weight[0]
    received = lax.all_to_all(outgoing, "grp", split_axis=0, concat_axis=0, tiled=True)
    leading = received.shape[0]
    count = received.shape[1]
    product = jnp.dot(
        received.reshape(leading * count, hidden_width), weight, preferred_element_type=jnp.float32
    )
    returned = lax.all_to_all(
        product.astype(jnp.bfloat16).reshape(leading, count, out_width),
        "grp",
        split_axis=0,
        concat_axis=0,
        tiled=True,
    )
    picked = returned[expert_ids, slot_index].reshape(tokens_here, top_slots, out_width)
    weighted = jnp.einsum("tk,tkd->td", gates, picked.astype(jnp.float32))
    mixed = shared_out.astype(jnp.float32) + weighted
    return mixed.astype(jnp.bfloat16)


def solution(mesh):
    in_specs = (
        P(("dom", "grp"), None),
        P(("dom", "grp"), None),
        P(("dom", "grp"), None, None),
        P("grp", None, None),
        P(("dom", "grp"), None),
    )
    out_specs = P(("dom", "grp"), None)
    return jax.shard_map(
        per_device, mesh=mesh, in_specs=in_specs, out_specs=out_specs, check_vma=False
    )
```

profile of v0, /device:TPU:15, one launch (start us, length us, event | category | flops | bytes accessed | tf_op | source)
XLA Modules:
  0.0 304.8 jit_solution(14467102816327067383)
XLA Ops:
  0.0 0.8 copy.6
  0.8 0.1 eq.29
  0.9 0.1 eq.25
  1.0 0.1 reshape.73
  1.1 1.2 reduce-window.6
  2.2 0.2 slice_reduce_fusion
  2.5 0.1 fusion.6
  2.6 0.3 broadcast_in_dim.2
  2.9 50.0 %scatter_fusion = bf16[16,64,1024]{2,1,0:T(8,128)(2,1)S(1)} fusion(bf16[16,64,1024]{2,1,0:T(8,128)(2,1)S(1)} %broadcast_in_dim.2, s32[512]{0:T(512)S(1)} %bitcast.39, bf16[512,1024]{1,0:T(8,128)(2,1)} %bitcast.42), kind=kCustom, calls=%fused_computation.1 | custom fusion | bytes 3149824 | tf_op jit(solution)/shard_map/scatter | solution.py:28
  52.9 53.7 %all_to_all.10 = bf16[16,64,1024]{2,1,0:T(8,128)(2,1)S(1)} all-to-all(bf16[16,64,1024]{2,1,0:T(8,128)(2,1)S(1)} %scatter_fusion), channel_id=1, replica_groups=mesh['dom'=2,'grp'=16] {'grp'}, dimensions={0} | all-to-all | bytes 4194304 | tf_op jit(solution)/shard_map/all_to_all | solution.py:31
  106.5 12.8 %convolution_convert_fusion = bf16[1024,3584]{1,0:T(8,128)(2,1)} fusion(bf16[1024,1024]{1,0:T(8,128)(2,1)S(1)} %bitcast.41, bf16[1,1024,3584]{2,1,0:T(8,128)(2,1)} %param.8), kind=kOutput, calls=%fused_computation.2 | convolution fusion | flops 7519862784 | bytes 16777216 | tf_op jit(solution)/shard_map/dot_general | solution.py:34
  119.3 0.0 copy-start.1
  119.3 5.3 %all-to-all-start.1 = ((bf16[16,64,3584]{2,1,0:T(8,128)(2,1)}), bf16[16,64,3584]{2,1,0:T(8,128)(2,1)}, u32[]{:S(2)}, u32[]{:S(2)}) async-start(bf16[16,64,3584]{2,1,0:T(8,128)(2,1)} %bitcast.40), calls=%async_computation.1 | async-start | bytes 14680064 | tf_op jit(solution)/shard_map/all_to_all | solution.py:37
  124.6 0.0 copy-done.1
  124.6 0.1 copy.10
  124.7 159.8 %all-to-all-done.1 = bf16[16,64,3584]{2,1,0:T(8,128)(2,1)} async-done(((bf16[16,64,3584]{2,1,0:T(8,128)(2,1)}), bf16[16,64,3584]{2,1,0:T(8,128)(2,1)}, u32[]{:S(2)}, u32[]{:S(2)}) %all-to-all-start.1) | async-done | bytes 7340064 | tf_op jit(solution)/shard_map/all_to_all | solution.py:37
  284.5 16.3 %gather_fusion = bf16[512,3584]{1,0:T(8,128)(2,1)} fusion(bf16[16,64,3584]{2,1,0:T(8,128)(2,1)} %all-to-all-done.1, s32[512]{0:T(512)S(1)} %bitcast.38), kind=kCustom, calls=%fused_computation | custom fusion | bytes 7344128 | tf_op jit(solution)/shard_map/gather | solution.py:44
  300.8 0.0 copy-start
  300.8 3.2 %fusion.1 = f32[64,1,3584]{2,1,0:T(1,128)S(1)} fusion(bf16[64,8,1]{1,2,0:T(2,128)(2,1)S(1)} %copy.10, bf16[512,3584]{1,0:T(8,128)(2,1)} %gather_fusion), kind=kOutput, calls=%fused_computation.4 | convolution fusion | flops 3670016 | bytes 4588544 | tf_op jit(solution)/shard_map/tk,tkd->td/dot_general | solution.py:45
  304.0 0.0 copy-done
  304.0 0.8 fusion.3
  (4 shorter events, 0.1 us)
Async XLA Ops:
  119.3 5.3 %copy-start.1 = (f32[64,8]{0,1:T(8,128)S(1)}, f32[64,8]{0,1:T(8,128)}, u32[]{:S(2)}) copy-start(f32[64,8]{0,1:T(8,128)} %param.6) | copy-start | bytes 6148
  119.3 165.1 %all-to-all-start.1 = ((bf16[16,64,3584]{2,1,0:T(8,128)(2,1)}), bf16[16,64,3584]{2,1,0:T(8,128)(2,1)}, u32[]{:S(2)}, u32[]{:S(2)}) async-start(bf16[16,64,3584]{2,1,0:T(8,128)(2,1)} %bitcast.40), calls=%async_computation.1 | async-start | bytes 14680064 | tf_op jit(solution)/shard_map/all_to_all | solution.py:37
  300.8 3.2 %copy-start = (bf16[64,3584]{1,0:T(8,128)(2,1)S(1)}, bf16[64,3584]{1,0:T(8,128)(2,1)}, u32[]{:S(2)}) copy-start(bf16[64,3584]{1,0:T(8,128)(2,1)} %param.9) | copy-start | bytes 1376260
where the time goes:
time: 308 us; the launch traced here: 305 us
  waiting for transfers between devices  160 us (52%)
  local copies, waits for them, and re-layouts  68 us (22%)
  blocking collectives  53.7 us (17%)
  matrix products  16 us (5%)
  starting transfers between devices  5.25 us (2%)
    all_to_all x1, waiting for transfers between devices, per_device(): lax.all_to_all(product.astype(jnp.bfloat16).reshape(leading, count, out_w...  160 us
    all_to_all x1, blocking collectives, per_device(): lax.all_to_all(outgoing, 'grp', split_axis=0, concat_axis=0, tiled=True)  53.7 us
    scatter x1, local copies, waits for them, and re-layouts, per_device(): outgoing = jnp.zeros((experts, capacity, hidden_width), jnp.bfloat16).at[...  50 us
    gather x1, local copies, waits for them, and re-layouts, per_device(): returned[expert_ids, slot_index].reshape(tokens_here, top_slots, out_width)  16.3 us
    dot_general x1, matrix products, per_device(): jnp.dot(received.reshape(leading * count, hidden_width), weight, preferre...  12.8 us
  transfers between devices with their start and end apart: 1, of which 1 were waited for; matrix products, arithmetic and copies ran while one was open for 0% of the time, Pallas kernels for 0%

commit v1 on v0

--- a/solution.py
+++ b/solution.py
@@ -7,15 +7,11 @@
 GROUP_DEV = 8
 
 
-def per_device(routes, gates, hidden, expert_weight, shared_out):
+def bucketed(routes, gates, hidden, expert_weight, shared_out, experts, capacity):
     tokens_here = routes.shape[0]
     top_slots = routes.shape[1]
     hidden_width = hidden.shape[2]
     out_width = expert_weight.shape[2]
-    experts = lax.axis_size("grp") * expert_weight.shape[0]
-    groups = lax.axis_size("grp") // GROUP_DEV
-    group_share = tokens_here * min(TOPG, groups) // groups
-    capacity = min(group_share, max(2, 2 * tokens_here * top_slots // experts))
     expert_ids = routes.reshape(-1)
     onehot = (expert_ids[:, None] == jnp.arange(experts, dtype=jnp.int32)[None, :]).astype(
         jnp.int32
@@ -47,6 +43,51 @@
     return mixed.astype(jnp.bfloat16)
 
 
+def gated_blocks(routes, gates, hidden, experts):
+    tokens, slots = routes.shape
+    width = hidden.shape[2]
+    ids = jnp.arange(experts, dtype=jnp.int32)
+    match = routes[None] == ids[:, None, None]
+    gate = jnp.sum(jnp.where(match, gates[None], 0.0), axis=2)
+    owner = jnp.arange(tokens, dtype=jnp.int32)
+    same = owner[:, None] == jnp.repeat(owner, slots)[None, :]
+    pick = match.reshape(experts, 1, tokens * slots) & same[None]
+    rows = jnp.dot(
+        pick.reshape(experts * tokens, tokens * slots).astype(jnp.bfloat16),
+        hidden.reshape(tokens * slots, width),
+        preferred_element_type=jnp.float32,
+    )
+    rows = rows * gate.reshape(experts * tokens, 1)
+    return rows.astype(jnp.bfloat16).reshape(experts, tokens, width)
+
+
+def dense(routes, gates, hidden, expert_weight, shared_out, experts):
+    tokens, width = routes.shape[0], hidden.shape[2]
+    blocks = gated_blocks(routes, gates, hidden, experts)
+    received = lax.all_to_all(blocks, "grp", split_axis=0, concat_axis=0, tiled=True)
+    product = jnp.dot(
+        received.reshape(experts * tokens, width),
+        expert_weight[0],
+        preferred_element_type=jnp.float32,
+    )
+    total = lax.psum_scatter(
+        product.astype(jnp.bfloat16), "grp", scatter_dimension=0, tiled=True
+    )
+    return (shared_out.astype(jnp.float32) + total.astype(jnp.float32)).astype(jnp.bfloat16)
+
+
+def per_device(routes, gates, hidden, expert_weight, shared_out):
+    tokens_here = routes.shape[0]
+    top_slots = routes.shape[1]
+    experts = lax.axis_size("grp") * expert_weight.shape[0]
+    groups = lax.axis_size("grp") // GROUP_DEV
+    group_share = tokens_here * min(TOPG, groups) // groups
+    capacity = min(group_share, max(2, 2 * tokens_here * top_slots // experts))
+    if capacity == tokens_here:
+        return dense(routes, gates, hidden, expert_weight, shared_out, experts)
+    return bucketed(routes, gates, hidden, expert_weight, shared_out, experts, capacity)
+
+
 def solution(mesh):
     in_specs = (
         P(("dom", "grp"), None),

time: 308 us -> 176 us (0.57)
  the two profiles are of different devices: /device:TPU:15 before, /device:TPU:0 now
where the time goes in v1:
time: 176 us
  waiting for transfers between devices  92.4 us (52%)
  blocking collectives  54.6 us (31%)
  between operations  13.5 us (8%)
  matrix products  11.1 us (6%)
  other arithmetic  2.95 us (2%)
    reduce_scatter x1, waiting for transfers between devices, dense(): lax.psum_scatter(product.astype(jnp.bfloat16), 'grp', scatter_dimension=0...  92.3 us
    all_to_all x1, blocking collectives, dense(): lax.all_to_all(blocks, 'grp', split_axis=0, concat_axis=0, tiled=True)  54.6 us
    dot_general x1, matrix products, dense(): jnp.dot(received.reshape(experts * tokens, width), expert_weight[0], pref...  9.8 us
  transfers between devices with their start and end apart: 1, of which 1 were waited for; matrix products, arithmetic and copies ran while one was open for 0% of the time, Pallas kernels for 0%

profile of v1, /device:TPU:0, one launch (start us, length us, event | category | flops | bytes accessed | tf_op | source)
XLA Modules:
  0.0 175.6 jit_solution(7590195456394279842)
XLA Ops:
  6.5 0.0 copy-start
  6.5 0.0 reduce-scatter.2.cloned.1.call-start
  6.5 0.9 copy.11
  7.4 0.7 select_reduce_fusion
  8.1 0.1 mul.10
  8.2 0.1 eq.44
  8.3 0.1 eq.49
  8.4 0.0 slice-start
  8.5 0.3 broadcast_and_fusion
  8.7 0.0 copy-done
  8.8 0.0 slice-start.1
  8.8 1.3 multiply_convert_fusion
  10.0 54.6 %all_to_all.5 = bf16[16,64,1024]{2,1,0:T(8,128)(2,1)S(1)} all-to-all(bf16[16,64,1024]{2,1,0:T(8,128)(2,1)S(1)} %bitcast.11), channel_id=1, replica_groups=mesh['dom'=2,'grp'=16] {'grp'}, dimensions={0} | all-to-all | bytes 4194304 | tf_op jit(solution)/shard_map/all_to_all | solution.py:67
  64.6 0.0 slice-done
  64.6 0.0 slice-done.1
  64.6 9.8 %convolution_convert_fusion = bf16[1024,3584]{1,0:T(8,128)(2,1)} fusion(bf16[1024,1024]{1,0:T(8,128)(2,1)S(1)} %bitcast.12, bf16[1,1024,3584]{2,1,0:T(8,128)(2,1)S(1)} %bitcast.15), kind=kOutput, calls=%fused_computation | convolution fusion | flops 7519862784 | bytes 16777216 | tf_op jit(solution)/shard_map/dot_general | solution.py:68
  74.5 0.0 copy-start.1
  74.5 0.0 reduce-scatter.2.cloned.1.call-update
  74.5 92.3 %reduce-scatter.2.cloned.1.call-done = bf16[64,3584]{1,0:T(8,128)(2,1)} async-done(((bf16[1024,3584]{1,0:T(8,128)(2,1)}), bf16[64,3584]{1,0:T(8,128)(2,1)}) %reduce-scatter.2.cloned.1.call-update) | async-done | bytes 458768 | tf_op jit(solution)/shard_map/reduce_scatter | solution.py:73
  166.8 0.0 copy-done.1
  166.8 1.9 %add_convert_fusion = bf16[64,3584]{1,0:T(8,128)(2,1)} fusion(bf16[64,3584]{1,0:T(8,128)(2,1)} %reduce-scatter.2.cloned.1.call-done, bf16[64,3584]{1,0:T(8,128)(2,1)S(1)} %copy-done.1), kind=kLoop, calls=%fused_computation.5 | loop fusion | flops 917504 | bytes 1376256 | tf_op jit(solution)/shard_map/convert_element_type | solution.py:76
  (4 shorter events, 0.0 us)
Async XLA Ops:
  6.5 2.2 %copy-start = (bf16[64,8,1024]{2,1,0:T(8,128)(2,1)S(1)}, bf16[64,8,1024]{2,1,0:T(8,128)(2,1)}, u32[]{:S(2)}) copy-start(bf16[64,8,1024]{2,1,0:T(8,128)(2,1)} %param.7) | copy-start | bytes 3145732
  6.5 160.3 %reduce-scatter.2.cloned.1.call-start = ((), (), s32[]{:S(2)}) async-start(), calls=%async_computation.2 | async-start | bytes 7798784 | tf_op jit(solution)/shard_map/reduce_scatter | solution.py:73
  8.4 56.2 %slice-start = ((s8[7340032]{0:T(1024)(128)(4,1)}), s8[4194304]{0:T(1024)(128)(4,1)S(1)}, s32[]{:S(2)}) async-start(s8[7340032]{0:T(1024)(128)(4,1)} %bitcast.14), calls=%async_computation.3 | async-start | bytes 8388608
  8.8 55.9 %slice-start.1 = ((s8[7340032]{0:T(1024)(128)(4,1)}), s8[3145728]{0:T(1024)(128)(4,1)S(1)}, s32[]{:S(2)}) async-start(s8[7340032]{0:T(1024)(128)(4,1)} %bitcast.14), calls=%async_computation.4 | async-start | bytes 6291456
  74.5 92.4 %copy-start.1 = (bf16[64,3584]{1,0:T(8,128)(2,1)S(1)}, bf16[64,3584]{1,0:T(8,128)(2,1)}, u32[]{:S(2)}) copy-start(bf16[64,3584]{1,0:T(8,128)(2,1)} %param.9) | copy-start | bytes 1376260
Sparse Core Ops, SparseCore 0:
  74.6 92.1 reduce-scatter.1

commit v2 on v1

--- a/solution.py
+++ b/solution.py
@@ -1,6 +1,8 @@
 import jax
 import jax.numpy as jnp
 from jax import lax
+from jax.experimental import pallas as pl
+from jax.experimental.pallas import tpu as pltpu
 from jax.sharding import PartitionSpec as P
 
 TOPG = 4
@@ -61,19 +63,308 @@
     return rows.astype(jnp.bfloat16).reshape(experts, tokens, width)
 
 
+CHUNKS = 7
+ORDER = (0, 1, 3, 2)
+
+
+def place(index):
+    return index // 4, (index // 2) % 2, index % 2
+
+
+def exchange_kernel(
+    blocks_ref,
+    w_hbm,
+    shared_ref,
+    out_ref,
+    w_ref,
+    rows,
+    part,
+    core_in,
+    x_in,
+    z_in,
+    w_sem,
+    own_sem,
+    disp_send,
+    disp_recv,
+    core_send,
+    core_recv,
+    x_send,
+    x_recv,
+    z_send,
+    z_recv,
+):
+    experts, tokens, width = blocks_ref.shape
+    cw = out_ref.shape[1] // CHUNKS
+    me = lax.axis_index("grp")
+    z, x, c = place(me)
+    partner = me + 1 - 2 * c
+    across = me + 2 - 4 * x
+
+    def far_z(s):
+        if s == 0:
+            return z
+        if s == 1:
+            return z + 1 - 2 * (z % 2)
+        if s == 2:
+            return (z + 2) % 4
+        return 3 - z
+
+    w_copy = pltpu.make_async_copy(w_hbm, w_ref, w_sem)
+    w_copy.start()
+    my_slot = c * 2 + x
+    own_copy = pltpu.make_async_copy(blocks_ref.at[me], rows.at[z, my_slot], own_sem)
+    own_copy.start()
+
+    barrier = pltpu.get_barrier_semaphore()
+    for i in range(1, experts):
+        pl.semaphore_signal(
+            barrier,
+            inc=1,
+            device_id={"grp": (me + i) % experts},
+            device_id_type=pl.DeviceIdType.MESH,
+        )
+    pl.semaphore_wait(barrier, experts - 1)
+
+    def dispatch_to(s, dx, dc):
+        ox = 1 - x if dx else x
+        oc = 1 - c if dc else c
+        oz = far_z(s)
+        other = oz * 4 + ox * 2 + oc
+        sent = pltpu.make_async_remote_copy(
+            src_ref=blocks_ref.at[other],
+            dst_ref=rows.at[z, my_slot],
+            send_sem=disp_send.at[s, dx * 2 + dc],
+            recv_sem=disp_recv.at[s, dx * 2 + dc],
+            device_id={"grp": other},
+            device_id_type=pl.DeviceIdType.MESH,
+        )
+        came = pltpu.make_async_remote_copy(
+            src_ref=blocks_ref.at[other],
+            dst_ref=rows.at[oz, oc * 2 + ox],
+            send_sem=disp_send.at[s, dx * 2 + dc],
+            recv_sem=disp_recv.at[s, dx * 2 + dc],
+            device_id={"grp": other},
+            device_id_type=pl.DeviceIdType.MESH,
+        )
+        return sent, came
+
+    def members(s):
+        return [(dx, dc) for dx in (0, 1) for dc in (0, 1) if s or dx or dc]
+
+    for dx, dc in members(0):
+        dispatch_to(0, dx, dc)[0].start()
+    for dx, dc in members(1):
+        dispatch_to(1, dx, dc)[0].start()
+        dispatch_to(3, dx, dc)[0].start()
+    for dx, dc in members(2):
+        dispatch_to(2, dx, dc)[0].start()
+
+    def columns(j):
+        return pl.ds(pl.multiple_of(j * cw, 128), cw)
+
+    def core_copy(s, j):
+        return pltpu.make_async_remote_copy(
+            src_ref=part.at[s, j, 1 - c],
+            dst_ref=core_in.at[s, j],
+            send_sem=core_send.at[s, j],
+            recv_sem=core_recv.at[s, j],
+            device_id={"grp": partner},
+            device_id_type=pl.DeviceIdType.MESH,
+        )
+
+    def x_copy(s, j):
+        return pltpu.make_async_remote_copy(
+            src_ref=part.at[s, j, c, 1 - x],
+            dst_ref=x_in.at[s, j],
+            send_sem=x_send.at[s, j],
+            recv_sem=x_recv.at[s, j],
+            device_id={"grp": across},
+            device_id_type=pl.DeviceIdType.MESH,
+        )
+
+    def z_copy(s, j):
+        goal = far_z(s)
+        up = goal > z
+        step = jnp.where(up, 1, -1)
+        nxt = z + step
+        slot = jnp.where(jnp.logical_and(nxt == goal, jnp.logical_not(up)), 4, goal)
+        return pltpu.make_async_remote_copy(
+            src_ref=part.at[s, j, c, x],
+            dst_ref=z_in.at[slot, j],
+            send_sem=z_send.at[s, j],
+            recv_sem=z_recv.at[slot, j],
+            device_id={"grp": me + 4 * step},
+            device_id_type=pl.DeviceIdType.MESH,
+        )
+
+    def z_arrival(slot, j):
+        return pltpu.make_async_remote_copy(
+            src_ref=z_in.at[slot, j],
+            dst_ref=z_in.at[slot, j],
+            send_sem=z_send.at[1, j],
+            recv_sem=z_recv.at[slot, j],
+            device_id={"grp": partner},
+            device_id_type=pl.DeviceIdType.MESH,
+        )
+
+    f32 = jnp.float32
+
+    def multiply(s):
+        for dx, dc in members(s):
+            dispatch_to(s, dx, dc)[1].wait_recv()
+        if s == 0:
+            own_copy.wait()
+            w_copy.wait()
+        goal = far_z(s)
+
+        @pl.loop(0, CHUNKS)
+        def _(j):
+            lhs = rows[goal].reshape(4 * tokens, width)
+            res = jnp.dot(lhs, w_ref[:, columns(j)], preferred_element_type=f32)
+            part[s, j] = res.astype(jnp.bfloat16).reshape(2, 2, tokens, cw)
+            core_copy(s, j).start()
+
+    def add_core(s):
+        @pl.loop(0, CHUNKS)
+        def _(j):
+            core_copy(s, j).wait_recv()
+            part[s, j, c, 1 - x] = (
+                part[s, j, c, 1 - x].astype(f32) + core_in[s, j, 1 - x].astype(f32)
+            ).astype(jnp.bfloat16)
+            x_copy(s, j).start()
+            part[s, j, c, x] = (
+                part[s, j, c, x].astype(f32) + core_in[s, j, x].astype(f32)
+            ).astype(jnp.bfloat16)
+
+    def add_x(s, j):
+        x_copy(s, j).wait_recv()
+        part[s, j, c, x] = (
+            part[s, j, c, x].astype(f32) + x_in[s, j].astype(f32)
+        ).astype(jnp.bfloat16)
+
+    def forward(s, j):
+        z_arrival(far_z(s), j).wait_recv()
+        part[s, j, c, x] = (
+            part[s, j, c, x].astype(f32) + z_in[far_z(s), j].astype(f32)
+        ).astype(jnp.bfloat16)
+        z_copy(s, j).start()
+
+    def handed(s):
+        up = far_z(s) > z
+        return jnp.logical_or(
+            jnp.logical_and(up, z > 0), jnp.logical_and(jnp.logical_not(up), z < 3)
+        )
+
+    def stage_x(s):
+        @pl.loop(0, CHUNKS)
+        def _(j):
+            add_x(s, j)
+            if s:
+                @pl.when(jnp.logical_not(handed(s)))
+                def _():
+                    z_copy(s, j).start()
+
+    def stage_z(s):
+        @pl.when(handed(s))
+        def _():
+            @pl.loop(0, CHUNKS)
+            def _(j):
+                forward(s, j)
+
+    multiply(0)
+    add_core(0)
+    multiply(1)
+    add_core(1)
+    stage_x(0)
+    multiply(3)
+    add_core(3)
+    stage_x(1)
+    stage_x(3)
+    multiply(2)
+    add_core(2)
+
+    @pl.loop(0, CHUNKS)
+    def _(j):
+        add_x(2, j)
+
+        @pl.when(jnp.logical_not(handed(2)))
+        def _():
+            z_copy(2, j).start()
+
+        @pl.when(handed(2))
+        def _():
+            forward(2, j)
+
+    stage_z(3)
+    stage_z(1)
+
+    @pl.loop(0, CHUNKS)
+    def _(j):
+        @pl.when(z > 0)
+        def _():
+            z_arrival(z, j).wait_recv()
+
+        @pl.when(z < 3)
+        def _():
+            z_arrival(4, j).wait_recv()
+
+        total = shared_ref[:, columns(j)].astype(f32) + part[0, j, c, x].astype(f32)
+        low = z_in[z, j].astype(f32)
+        high = z_in[4, j].astype(f32)
+        total = total + jnp.where(z > 0, low, 0.0) + jnp.where(z < 3, high, 0.0)
+        out_ref[:, columns(j)] = total.astype(jnp.bfloat16)
+
+    for s in ORDER:
+        for dx, dc in members(s):
+            dispatch_to(s, dx, dc)[0].wait_send()
+
+        @pl.loop(0, CHUNKS)
+        def _(j):
+            core_copy(s, j).wait_send()
+            x_copy(s, j).wait_send()
+            if s:
+                z_copy(s, j).wait_send()
+
+
 def dense(routes, gates, hidden, expert_weight, shared_out, experts):
     tokens, width = routes.shape[0], hidden.shape[2]
+    out_width = expert_weight.shape[2]
+    cw = out_width // CHUNKS
     blocks = gated_blocks(routes, gates, hidden, experts)
-    received = lax.all_to_all(blocks, "grp", split_axis=0, concat_axis=0, tiled=True)
-    product = jnp.dot(
-        received.reshape(experts * tokens, width),
-        expert_weight[0],
-        preferred_element_type=jnp.float32,
-    )
-    total = lax.psum_scatter(
-        product.astype(jnp.bfloat16), "grp", scatter_dimension=0, tiled=True
-    )
-    return (shared_out.astype(jnp.float32) + total.astype(jnp.float32)).astype(jnp.bfloat16)
+    dma = pltpu.SemaphoreType.DMA
+    vmem = pl.BlockSpec(memory_space=pltpu.VMEM)
+    return pl.pallas_call(
+        exchange_kernel,
+        out_shape=jax.ShapeDtypeStruct((tokens, out_width), jnp.bfloat16),
+        in_specs=[vmem, pl.BlockSpec(memory_space=pl.ANY), vmem],
+        out_specs=vmem,
+        scratch_shapes=[
+            pltpu.VMEM((width, out_width), jnp.bfloat16),
+            pltpu.VMEM((4, 4, tokens, width), jnp.bfloat16),
+            pltpu.VMEM((4, CHUNKS, 2, 2, tokens, cw), jnp.bfloat16),
+            pltpu.VMEM((4, CHUNKS, 2, tokens, cw), jnp.bfloat16),
+            pltpu.VMEM((4, CHUNKS, tokens, cw), jnp.bfloat16),
+            pltpu.VMEM((5, CHUNKS, tokens, cw), jnp.bfloat16),
+            dma,
+            dma,
+            dma((4, 4)),
+            dma((4, 4)),
+            dma((4, CHUNKS)),
+            dma((4, CHUNKS)),
+            dma((4, CHUNKS)),
+            dma((4, CHUNKS)),
+            dma((4, CHUNKS)),
+            dma((5, CHUNKS)),
+        ],
+        compiler_params=pltpu.CompilerParams(
+            collective_id=0, has_side_effects=True, vmem_limit_bytes=48 * 1024 * 1024
+        ),
+        cost_estimate=pl.CostEstimate(
+            flops=2 * experts * tokens * width * out_width,
+            bytes_accessed=2 * width * out_width,
+            transcendentals=0,
+        ),
+    )(blocks, expert_weight[0], shared_out)
 
 
 def per_device(routes, gates, hidden, expert_weight, shared_out):
@@ -83,7 +374,7 @@
     groups = lax.axis_size("grp") // GROUP_DEV
     group_share = tokens_here * min(TOPG, groups) // groups
     capacity = min(group_share, max(2, 2 * tokens_here * top_slots // experts))
-    if capacity == tokens_here:
+    if capacity == tokens_here and experts == 16:
         return dense(routes, gates, hidden, expert_weight, shared_out, experts)
     return bucketed(routes, gates, hidden, expert_weight, shared_out, experts, capacity)
 

time: 176 us -> 100 us (0.57)
  Pallas kernels: 0 us -> 95.7 us
  waiting for transfers between devices: 92.4 us -> 0 us
  blocking collectives: 54.6 us -> 0 us
  between operations: 13.5 us -> 0.07 us
  matrix products: 11.1 us -> 1.25 us
  other arithmetic: 2.95 us -> 1.14 us
    pallas_call x0 -> x1, Pallas kernels: none -> 95.7 us  [dense(): pl.pallas_call(exchange_kernel, out_shape=jax.ShapeDtypeStruct((tokens, o...]
    reduce_scatter x1 -> x0, waiting for transfers between devices: 92.3 us -> none  [dense(): lax.psum_scatter(product.astype(jnp.bfloat16), 'grp', scatter_dimension=0...]
    all_to_all x1 -> x0, blocking collectives: 54.6 us -> none  [dense(): lax.all_to_all(blocks, 'grp', split_axis=0, concat_axis=0, tiled=True)]
    dot_general x1 -> x0, matrix products: 9.8 us -> none  [dense(): jnp.dot(received.reshape(experts * tokens, width), expert_weight[0], pref...]
    convert_element_type x1 -> x0, other arithmetic: 1.89 us -> none  [dense(): (shared_out.astype(jnp.float32) + total.astype(jnp.float32)).astype(jnp.b...]
  transfers between devices with their start and end apart: 1 -> 0, of which waited for: 1 -> 0; matrix products, arithmetic and copies ran while one was open for 0% -> 0% of each run, Pallas kernels for 0% -> 0%
where the time goes in v2:
time: 100 us
  Pallas kernels  95.7 us (96%)
  local copies, waits for them, and re-layouts  1.81 us (2%)
  matrix products  1.25 us (1%)
  other arithmetic  1.14 us (1%)
    pallas_call x1, Pallas kernels, dense(): pl.pallas_call(exchange_kernel, out_shape=jax.ShapeDtypeStruct((tokens, o...  95.7 us

profile of v2, /device:TPU:0, one launch (start us, length us, event | category | flops | bytes accessed | tf_op | source)
XLA Modules:
  0.0 100.0 jit_solution(2778824396678722744)
XLA Ops:
  0.0 0.0 copy-start
  0.0 0.8 select_reduce_fusion
  0.8 0.1 mul.10
  0.9 0.8 copy.11
  1.7 0.1 eq.44
  1.8 0.1 eq.49
  1.9 0.3 broadcast_and_fusion
  2.2 0.0 copy-done
  2.2 0.0 copy-start.1
  2.2 1.3 %multiply_convert_fusion = bf16[1024,1024]{1,0:T(8,128)(2,1)S(1)} fusion(pred[1024,512]{1,0:T(32,128)(4,1)S(1)} %bitcast.8, f32[1024]{0:T(1024)S(1)} %mul.10, bf16[64,8,1024]{2,1,0:T(8,128)(2,1)S(1)} %copy-done), kind=kOutput, calls=%fused_computation | convolution fusion | flops 1075838976 | bytes 3674112 | tf_op jit(solution)/shard_map/dot_general | solution.py:57
  3.5 0.0 copy-done.1
  3.5 95.7 %shard_map.55 = bf16[64,3584]{1,0:T(8,128)(2,1)S(1)} custom-call(bf16[16,64,1024]{2,1,0:T(8,128)(2,1)S(1)} %bitcast.7, bf16[1024,3584]{1,0:T(8,128)(2,1)} %bitcast.9, bf16[64,3584]{1,0:T(8,128)(2,1)S(1)} %copy-done.1), custom_call_target="tpu_custom_call" | custom-call | flops 7516192768 | bytes 7340032 | tf_op jit(solution)/shard_map/pallas_call | solution.py:336
  99.2 0.8 copy.15
  (3 shorter events, 0.0 us)
Async XLA Ops:
  0.0 2.2 %copy-start = (bf16[64,8,1024]{2,1,0:T(8,128)(2,1)S(1)}, bf16[64,8,1024]{2,1,0:T(8,128)(2,1)}, u32[]{:S(2)}) copy-start(bf16[64,8,1024]{2,1,0:T(8,128)(2,1)} %param.7) | copy-start | bytes 3145732
  2.2 1.3 %copy-start.1 = (bf16[64,3584]{1,0:T(8,128)(2,1)S(1)}, bf16[64,3584]{1,0:T(8,128)(2,1)}, u32[]{:S(2)}) copy-start(bf16[64,3584]{1,0:T(8,128)(2,1)} %shared_ref.1) | copy-start | bytes 1376260

commit v3 on v2

--- a/solution.py
+++ b/solution.py
@@ -45,26 +45,8 @@
     return mixed.astype(jnp.bfloat16)
 
 
-def gated_blocks(routes, gates, hidden, experts):
-    tokens, slots = routes.shape
-    width = hidden.shape[2]
-    ids = jnp.arange(experts, dtype=jnp.int32)
-    match = routes[None] == ids[:, None, None]
-    gate = jnp.sum(jnp.where(match, gates[None], 0.0), axis=2)
-    owner = jnp.arange(tokens, dtype=jnp.int32)
-    same = owner[:, None] == jnp.repeat(owner, slots)[None, :]
-    pick = match.reshape(experts, 1, tokens * slots) & same[None]
-    rows = jnp.dot(
-        pick.reshape(experts * tokens, tokens * slots).astype(jnp.bfloat16),
-        hidden.reshape(tokens * slots, width),
-        preferred_element_type=jnp.float32,
-    )
-    rows = rows * gate.reshape(experts * tokens, 1)
-    return rows.astype(jnp.bfloat16).reshape(experts, tokens, width)
-
-
 CHUNKS = 7
-ORDER = (0, 1, 3, 2)
+PHASES = (0, 1, 2, 3)
 
 
 def place(index):
@@ -72,18 +54,20 @@
 
 
 def exchange_kernel(
-    blocks_ref,
+    routes_ref,
+    gates_ref,
+    hidden_ref,
     w_hbm,
     shared_ref,
     out_ref,
     w_ref,
+    blocks_ref,
     rows,
     part,
     core_in,
     x_in,
     z_in,
     w_sem,
-    own_sem,
     disp_send,
     disp_recv,
     core_send,
@@ -94,26 +78,27 @@
     z_recv,
 ):
     experts, tokens, width = blocks_ref.shape
+    slots = hidden_ref.shape[0] // tokens
     cw = out_ref.shape[1] // CHUNKS
+    f32 = jnp.float32
     me = lax.axis_index("grp")
     z, x, c = place(me)
     partner = me + 1 - 2 * c
     across = me + 2 - 4 * x
+    outer = jnp.logical_or(z == 0, z == 3)
 
     def far_z(s):
         if s == 0:
             return z
         if s == 1:
             return z + 1 - 2 * (z % 2)
+        low = z < 2
         if s == 2:
-            return (z + 2) % 4
-        return 3 - z
+            return jnp.where(low, 3, 0)
+        return jnp.where(low, 2, 1)
 
     w_copy = pltpu.make_async_copy(w_hbm, w_ref, w_sem)
     w_copy.start()
-    my_slot = c * 2 + x
-    own_copy = pltpu.make_async_copy(blocks_ref.at[me], rows.at[z, my_slot], own_sem)
-    own_copy.start()
 
     barrier = pltpu.get_barrier_semaphore()
     for i in range(1, experts):
@@ -123,41 +108,74 @@
             device_id={"grp": (me + i) % experts},
             device_id_type=pl.DeviceIdType.MESH,
         )
-    pl.semaphore_wait(barrier, experts - 1)
-
-    def dispatch_to(s, dx, dc):
+
+    def make_blocks(oz):
+        shape = (tokens, tokens * slots)
+        token = lax.broadcasted_iota(jnp.int32, shape, 0)
+        same = token == lax.broadcasted_iota(jnp.int32, shape, 1) // slots
+        picks, scales = [], []
+        for i in range(4):
+            pick = jnp.where(
+                jnp.logical_and(same, routes_ref[...] == oz * 4 + i), 1.0, 0.0
+            )
+            scales.append(jnp.sum(pick * gates_ref[...], axis=1, keepdims=True))
+            picks.append(pick.astype(jnp.bfloat16))
+        made = jnp.dot(
+            jnp.concatenate(picks, axis=0), hidden_ref[...], preferred_element_type=f32
+        )
+        made = made * jnp.concatenate(scales, axis=0)
+        blocks_ref[pl.ds(oz * 4, 4)] = made.astype(jnp.bfloat16).reshape(4, tokens, width)
+
+    my_slot = c * 2 + x
+
+    def send_to(oz, dx, dc):
         ox = 1 - x if dx else x
         oc = 1 - c if dc else c
-        oz = far_z(s)
         other = oz * 4 + ox * 2 + oc
-        sent = pltpu.make_async_remote_copy(
+        return pltpu.make_async_remote_copy(
             src_ref=blocks_ref.at[other],
             dst_ref=rows.at[z, my_slot],
-            send_sem=disp_send.at[s, dx * 2 + dc],
-            recv_sem=disp_recv.at[s, dx * 2 + dc],
+            send_sem=disp_send.at[oz, oc * 2 + ox],
+            recv_sem=disp_recv.at[z, my_slot],
             device_id={"grp": other},
             device_id_type=pl.DeviceIdType.MESH,
         )
-        came = pltpu.make_async_remote_copy(
-            src_ref=blocks_ref.at[other],
+
+    def arrival(oz, dx, dc):
+        ox = 1 - x if dx else x
+        oc = 1 - c if dc else c
+        return pltpu.make_async_remote_copy(
+            src_ref=blocks_ref.at[me],
             dst_ref=rows.at[oz, oc * 2 + ox],
-            send_sem=disp_send.at[s, dx * 2 + dc],
-            recv_sem=disp_recv.at[s, dx * 2 + dc],
-            device_id={"grp": other},
-            device_id_type=pl.DeviceIdType.MESH,
-        )
-        return sent, came
+            send_sem=disp_send.at[oz, oc * 2 + ox],
+            recv_sem=disp_recv.at[oz, oc * 2 + ox],
+            device_id={"grp": oz * 4 + ox * 2 + oc},
+            device_id_type=pl.DeviceIdType.MESH,
+        )
 
     def members(s):
         return [(dx, dc) for dx in (0, 1) for dc in (0, 1) if s or dx or dc]
 
+    near_z = far_z(1)
+    across_z = (z + 2) % 4
+    other_z = 3 - z
+
+    def send_far():
+        for dx, dc in members(1):
+            send_to(other_z, dx, dc).start()
+            send_to(across_z, dx, dc).start()
+
+    make_blocks(z)
+    pl.semaphore_wait(barrier, experts - 1)
     for dx, dc in members(0):
-        dispatch_to(0, dx, dc)[0].start()
+        send_to(z, dx, dc).start()
+    rows[z, my_slot] = blocks_ref[me]
+    make_blocks(near_z)
     for dx, dc in members(1):
-        dispatch_to(1, dx, dc)[0].start()
-        dispatch_to(3, dx, dc)[0].start()
-    for dx, dc in members(2):
-        dispatch_to(2, dx, dc)[0].start()
+        send_to(near_z, dx, dc).start()
+    make_blocks(other_z)
+    make_blocks(across_z)
+    send_far()
 
     def columns(j):
         return pl.ds(pl.multiple_of(j * cw, 128), cw)
@@ -207,15 +225,12 @@
             device_id_type=pl.DeviceIdType.MESH,
         )
 
-    f32 = jnp.float32
-
     def multiply(s):
+        goal = far_z(s)
         for dx, dc in members(s):
-            dispatch_to(s, dx, dc)[1].wait_recv()
+            arrival(goal, dx, dc).wait_recv()
         if s == 0:
-            own_copy.wait()
             w_copy.wait()
-        goal = far_z(s)
 
         @pl.loop(0, CHUNKS)
         def _(j):
@@ -263,40 +278,31 @@
                 @pl.when(jnp.logical_not(handed(s)))
                 def _():
                     z_copy(s, j).start()
-
-    def stage_z(s):
-        @pl.when(handed(s))
-        def _():
-            @pl.loop(0, CHUNKS)
-            def _(j):
-                forward(s, j)
+            if s > 1:
+                @pl.when(handed(s))
+                def _():
+                    forward(s, j)
 
     multiply(0)
     add_core(0)
     multiply(1)
+
     add_core(1)
     stage_x(0)
+    multiply(2)
+    add_core(2)
+    stage_x(1)
+    stage_x(2)
     multiply(3)
     add_core(3)
-    stage_x(1)
+
+    @pl.when(handed(1))
+    def _():
+        @pl.loop(0, CHUNKS)
+        def _(j):
+            forward(1, j)
+
     stage_x(3)
-    multiply(2)
-    add_core(2)
-
-    @pl.loop(0, CHUNKS)
-    def _(j):
-        add_x(2, j)
-
-        @pl.when(jnp.logical_not(handed(2)))
-        def _():
-            z_copy(2, j).start()
-
-        @pl.when(handed(2))
-        def _():
-            forward(2, j)
-
-    stage_z(3)
-    stage_z(1)
 
     @pl.loop(0, CHUNKS)
     def _(j):
@@ -314,9 +320,9 @@
         total = total + jnp.where(z > 0, low, 0.0) + jnp.where(z < 3, high, 0.0)
         out_ref[:, columns(j)] = total.astype(jnp.bfloat16)
 
-    for s in ORDER:
+    for s in PHASES:
         for dx, dc in members(s):
-            dispatch_to(s, dx, dc)[0].wait_send()
+            send_to((z, near_z, across_z, other_z)[s], dx, dc).wait_send()
 
         @pl.loop(0, CHUNKS)
         def _(j):
@@ -330,22 +336,22 @@
     tokens, width = routes.shape[0], hidden.shape[2]
     out_width = expert_weight.shape[2]
     cw = out_width // CHUNKS
-    blocks = gated_blocks(routes, gates, hidden, experts)
+    slots = routes.shape[1]
     dma = pltpu.SemaphoreType.DMA
     vmem = pl.BlockSpec(memory_space=pltpu.VMEM)
     return pl.pallas_call(
         exchange_kernel,
         out_shape=jax.ShapeDtypeStruct((tokens, out_width), jnp.bfloat16),
-        in_specs=[vmem, pl.BlockSpec(memory_space=pl.ANY), vmem],
+        in_specs=[vmem, vmem, vmem, pl.BlockSpec(memory_space=pl.ANY), vmem],
         out_specs=vmem,
         scratch_shapes=[
             pltpu.VMEM((width, out_width), jnp.bfloat16),
+            pltpu.VMEM((experts, tokens, width), jnp.bfloat16),
             pltpu.VMEM((4, 4, tokens, width), jnp.bfloat16),
             pltpu.VMEM((4, CHUNKS, 2, 2, tokens, cw), jnp.bfloat16),
             pltpu.VMEM((4, CHUNKS, 2, tokens, cw), jnp.bfloat16),
             pltpu.VMEM((4, CHUNKS, tokens, cw), jnp.bfloat16),
             pltpu.VMEM((5, CHUNKS, tokens, cw), jnp.bfloat16),
-            dma,
             dma,
             dma((4, 4)),
             dma((4, 4)),
@@ -364,7 +370,13 @@
             bytes_accessed=2 * width * out_width,
             transcendentals=0,
         ),
-    )(blocks, expert_weight[0], shared_out)
+    )(
+        routes.reshape(1, tokens * slots),
+        gates.reshape(1, tokens * slots),
+        hidden.reshape(tokens * slots, width),
+        expert_weight[0],
+        shared_out,
+    )
 
 
 def per_device(routes, gates, hidden, expert_weight, shared_out):

time: 100 us -> 90.3 us (0.903)
  Pallas kernels: 95.7 us -> 85.3 us
  local copies, waits for them, and re-layouts: 1.81 us -> 4.73 us
  matrix products: 1.25 us -> 0 us
  other arithmetic: 1.14 us -> 0 us
    pallas_call x1, Pallas kernels: 95.7 us -> 85.3 us  [dense(): pl.pallas_call(exchange_kernel, out_shape=jax.ShapeDtypeStruct((tokens, o...]
    unnamed x6 -> x7, local copies, waits for them, and re-layouts: 1.55 us -> 4.55 us
    dot_general x1 -> x0, matrix products: 1.25 us -> none  [gated_blocks(): jnp.dot(pick.reshape(experts * tokens, tokens * slots).astype(jnp.bfloat1...]
where the time goes in v3:
time: 90.3 us; the launch traced here: 90.1 us
  Pallas kernels  85.3 us (94%)
  local copies, waits for them, and re-layouts  4.73 us (5%)
    pallas_call x1, Pallas kernels, dense(): pl.pallas_call(exchange_kernel, out_shape=jax.ShapeDtypeStruct((tokens, o...  85.3 us
    unnamed x7, local copies, waits for them, and re-layouts  4.55 us

profile of v3, /device:TPU:0, one launch (start us, length us, event | category | flops | bytes accessed | tf_op | source)
XLA Modules:
  0.0 90.1 jit_solution(7296298473899217877)
XLA Ops:
  0.0 0.8 copy.8
  0.8 0.1 reshape.9.routes_ref
  0.9 0.8 copy.9
  1.6 0.1 reshape.10.gates_ref
  1.7 0.0 copy-start
  1.7 1.2 %copy-done = bf16[64,8,1024]{2,1,0:T(8,128)(2,1)S(1)} copy-done((bf16[64,8,1024]{2,1,0:T(8,128)(2,1)S(1)}, bf16[64,8,1024]{2,1,0:T(8,128)(2,1)}, u32[]{:S(2)}) %copy-start) | copy-done | bytes 1048600
  3.0 0.0 copy-start.1
  3.0 1.0 %copy-done.1 = bf16[64,3584]{1,0:T(8,128)(2,1)S(1)} copy-done((bf16[64,3584]{1,0:T(8,128)(2,1)S(1)}, bf16[64,3584]{1,0:T(8,128)(2,1)}, u32[]{:S(2)}) %copy-start.1) | copy-done | bytes 458776
  4.0 85.3 %shard_map.55 = bf16[64,3584]{1,0:T(8,128)(2,1)S(1)} custom-call(s32[1,512]{1,0:T(1,128)S(1)} %reshape.9.routes_ref, f32[1,512]{1,0:T(1,128)S(1)} %reshape.10.gates_ref, bf16[512,1024]{1,0:T(8,128)(2,1)S(1)} %bitcast.2, bf16[1024,3584]{1,0:T(8,128)(2,1)} %bitcast.3, bf16[64,3584]{1,0:T(8,128)(2,1)S(1)} %copy-done.1), custom_call_target="tpu_custom_call" | custom-call | flops 7516192768 | bytes 7340032 | tf_op jit(solution)/shard_map/pallas_call | solution.py:342
  89.3 0.8 copy.11
Async XLA Ops:
  1.7 1.2 %copy-start = (bf16[64,8,1024]{2,1,0:T(8,128)(2,1)S(1)}, bf16[64,8,1024]{2,1,0:T(8,128)(2,1)}, u32[]{:S(2)}) copy-start(bf16[64,8,1024]{2,1,0:T(8,128)(2,1)} %param.7) | copy-start | bytes 3145732
  3.0 1.0 %copy-start.1 = (bf16[64,3584]{1,0:T(8,128)(2,1)S(1)}, bf16[64,3584]{1,0:T(8,128)(2,1)}, u32[]{:S(2)}) copy-start(bf16[64,3584]{1,0:T(8,128)(2,1)} %shared_ref.1) | copy-start | bytes 1376260

commit v4 on v3

--- a/solution.py
+++ b/solution.py
@@ -46,6 +46,7 @@
 
 
 CHUNKS = 7
+LAG = 2
 PHASES = (0, 1, 2, 3)
 
 
@@ -225,6 +226,16 @@
             device_id_type=pl.DeviceIdType.MESH,
         )
 
+    def add_core(s, j):
+        core_copy(s, j).wait_recv()
+        part[s, j, c, 1 - x] = (
+            part[s, j, c, 1 - x].astype(f32) + core_in[s, j, 1 - x].astype(f32)
+        ).astype(jnp.bfloat16)
+        x_copy(s, j).start()
+        part[s, j, c, x] = (
+            part[s, j, c, x].astype(f32) + core_in[s, j, x].astype(f32)
+        ).astype(jnp.bfloat16)
+
     def multiply(s):
         goal = far_z(s)
         for dx, dc in members(s):
@@ -232,24 +243,18 @@
         if s == 0:
             w_copy.wait()
 
-        @pl.loop(0, CHUNKS)
+        @pl.loop(0, CHUNKS + LAG)
         def _(j):
-            lhs = rows[goal].reshape(4 * tokens, width)
-            res = jnp.dot(lhs, w_ref[:, columns(j)], preferred_element_type=f32)
-            part[s, j] = res.astype(jnp.bfloat16).reshape(2, 2, tokens, cw)
-            core_copy(s, j).start()
-
-    def add_core(s):
-        @pl.loop(0, CHUNKS)
-        def _(j):
-            core_copy(s, j).wait_recv()
-            part[s, j, c, 1 - x] = (
-                part[s, j, c, 1 - x].astype(f32) + core_in[s, j, 1 - x].astype(f32)
-            ).astype(jnp.bfloat16)
-            x_copy(s, j).start()
-            part[s, j, c, x] = (
-                part[s, j, c, x].astype(f32) + core_in[s, j, x].astype(f32)
-            ).astype(jnp.bfloat16)
+            @pl.when(j < CHUNKS)
+            def _():
+                lhs = rows[goal].reshape(4 * tokens, width)
+                res = jnp.dot(lhs, w_ref[:, columns(j)], preferred_element_type=f32)
+                part[s, j] = res.astype(jnp.bfloat16).reshape(2, 2, tokens, cw)
+                core_copy(s, j).start()
+
+            @pl.when(j >= LAG)
+            def _():
+                add_core(s, j - LAG)
 
     def add_x(s, j):
         x_copy(s, j).wait_recv()
@@ -284,17 +289,12 @@
                     forward(s, j)
 
     multiply(0)
-    add_core(0)
     multiply(1)
 
-    add_core(1)
-    stage_x(0)
     multiply(2)
-    add_core(2)
     stage_x(1)
+    multiply(3)
     stage_x(2)
-    multiply(3)
-    add_core(3)
 
     @pl.when(handed(1))
     def _():
@@ -303,6 +303,7 @@
             forward(1, j)
 
     stage_x(3)
+    stage_x(0)
 
     @pl.loop(0, CHUNKS)
     def _(j):

time: 90.3 us -> 90.2 us (level); the launches traced: 90.1 us -> 88.6 us
  Pallas kernels: 85.3 us -> 83.8 us
    pallas_call x1, Pallas kernels: 85.3 us -> 83.8 us  [dense(): pl.pallas_call(exchange_kernel, out_shape=jax.ShapeDtypeStruct((tokens, o...]
where the time goes in v4:
time: 90.2 us; the launch traced here: 88.6 us
  Pallas kernels  83.8 us (93%)
  local copies, waits for them, and re-layouts  4.73 us (5%)
    pallas_call x1, Pallas kernels, dense(): pl.pallas_call(exchange_kernel, out_shape=jax.ShapeDtypeStruct((tokens, o...  83.8 us
    unnamed x7, local copies, waits for them, and re-layouts  4.55 us

profile of v4, /device:TPU:0, one launch (start us, length us, event | category | flops | bytes accessed | tf_op | source)
XLA Modules:
  0.0 88.6 jit_solution(9942605521205466277)
XLA Ops:
  0.0 0.8 copy.8
  0.8 0.1 reshape.9.routes_ref
  0.9 0.8 copy.9
  1.6 0.1 reshape.10.gates_ref
  1.7 0.0 copy-start
  1.7 1.2 %copy-done = bf16[64,8,1024]{2,1,0:T(8,128)(2,1)S(1)} copy-done((bf16[64,8,1024]{2,1,0:T(8,128)(2,1)S(1)}, bf16[64,8,1024]{2,1,0:T(8,128)(2,1)}, u32[]{:S(2)}) %copy-start) | copy-done | bytes 1048600
  3.0 0.0 copy-start.1
  3.0 1.0 %copy-done.1 = bf16[64,3584]{1,0:T(8,128)(2,1)S(1)} copy-done((bf16[64,3584]{1,0:T(8,128)(2,1)S(1)}, bf16[64,3584]{1,0:T(8,128)(2,1)}, u32[]{:S(2)}) %copy-start.1) | copy-done | bytes 458776
  4.0 83.8 %shard_map.55 = bf16[64,3584]{1,0:T(8,128)(2,1)S(1)} custom-call(s32[1,512]{1,0:T(1,128)S(1)} %reshape.9.routes_ref, f32[1,512]{1,0:T(1,128)S(1)} %reshape.10.gates_ref, bf16[512,1024]{1,0:T(8,128)(2,1)S(1)} %bitcast.2, bf16[1024,3584]{1,0:T(8,128)(2,1)} %bitcast.3, bf16[64,3584]{1,0:T(8,128)(2,1)S(1)} %copy-done.1), custom_call_target="tpu_custom_call" | custom-call | flops 7516192768 | bytes 7340032 | tf_op jit(solution)/shard_map/pallas_call | solution.py:343
  87.8 0.8 copy.11
Async XLA Ops:
  1.7 1.2 %copy-start = (bf16[64,8,1024]{2,1,0:T(8,128)(2,1)S(1)}, bf16[64,8,1024]{2,1,0:T(8,128)(2,1)}, u32[]{:S(2)}) copy-start(bf16[64,8,1024]{2,1,0:T(8,128)(2,1)} %param.7) | copy-start | bytes 3145732
  3.0 1.0 %copy-start.1 = (bf16[64,3584]{1,0:T(8,128)(2,1)S(1)}, bf16[64,3584]{1,0:T(8,128)(2,1)}, u32[]{:S(2)}) copy-start(bf16[64,3584]{1,0:T(8,128)(2,1)} %shared_ref.1) | copy-start | bytes 1376260
